TPU v7x, 1024 devices: a whole 8x8x8 slice. The times are simulated.
1024 devices in a mesh: rep: 64 (over x_hi, z, core), fsdp: 16 (over y, x_lo).
Axes of the slice: x: 8 (x_hi: 4, x_lo: 2; x = x_hi * 2 + x_lo), y: 8, z: 8, core: 2. Of those that a mesh axis runs over, the one named last changes fastest.
Arguments:
- tokens: bfloat16 [131072, 3072], P(('rep', 'fsdp')), may hold values from -6 to 6
- cotangent: bfloat16 [131072, 1024], P(('rep', 'fsdp')), may hold values from -0.13258252 to 0.13258252
- norm_gain: float32 [3072], replicated, may hold values from 0.5 to 9.2, as said below
- replica_drift: float32 [64, 3072, 1024], P('rep', 'fsdp'), may hold values from -3 to 3
- exponents: int32 [64, 3072, 8], P('rep', 'fsdp'), may hold values from 1 to 3
- global_weight: float32 [3072, 1024], P('fsdp'), may hold values from -6 to 6
- momentum: float32 [16, 64, 3, 1024], P('fsdp', 'rep'), may hold values from -3 to 3
Outputs:
- new_global: float32 [3072, 1024], P('fsdp')
- new_momentum: float32 [16, 64, 3, 1024], P('fsdp', 'rep')
Inputs may be any that keep to these rules, and one draw needn't show every extreme that they name: `norm_gain`: positive gains.
All inputs are finite; a program needn't handle non-finite values.
Results may differ from a plain program's by a relative error of at most 0.005.
Values may be sent and summed in bfloat16 or wider, within the bound.
A program may use at most 32 MiB of HBM per device.

v0:
```python
import jax
import jax.numpy as jnp
from jax import lax
from jax.sharding import PartitionSpec as P

inner_rate = 0.5
outer_rate = 0.7
momentum_decay = 0.9
code_limit = 7.0


def sylvester(length):
    row_index = jnp.arange(length, dtype=jnp.int32)[:, None]
    col_index = jnp.arange(length, dtype=jnp.int32)[None, :]
    parity = jnp.zeros((length, length), jnp.int32)
    for bit_pos in range(length.bit_length() - 1):
        parity = parity + (
            jnp.right_shift(row_index, bit_pos) & jnp.right_shift(col_index, bit_pos) & 1
        )
    return jnp.where(parity % 2 == 0, 1.0, -1.0).astype(jnp.float32)


def body(tokens, cotangent, norm_gain, replica_drift, exponents, global_weight, momentum):
    model_width = tokens.shape[1]
    columns = cotangent.shape[1]
    head_count = exponents.shape[2]
    head_size = columns // head_count
    shard_rows = global_weight.shape[0]
    widened = tokens.astype(jnp.float32)
    mean_square = jnp.mean(widened * widened, axis=-1, keepdims=True)
    normed = (widened * lax.rsqrt(mean_square + 1e-06) * norm_gain).astype(jnp.bfloat16)
    gradient = lax.psum_scatter(
        lax.dot_general(
            normed, cotangent, (((0,), (0,)), ((), ())), preferred_element_type=jnp.float32
        ).astype(jnp.bfloat16),
        "fsdp",
        scatter_dimension=0,
        tiled=True,
    ).astype(jnp.float32)
    square = lax.psum(jnp.sum(gradient * gradient), "fsdp")
    factor = jnp.minimum(1.0, 1.0 / jnp.sqrt(square / (model_width * columns) + 1e-06))
    pseudo_grad = replica_drift[0] + inner_rate * factor * gradient
    sign_table = sylvester(head_size)
    sign_low = sign_table.astype(jnp.bfloat16)
    unit_scale = head_size ** (-0.5)
    blocks = pseudo_grad.reshape(shard_rows * head_count, head_size)
    turned = jnp.dot(blocks, sign_table, precision=lax.Precision.HIGHEST) * unit_scale
    expo_float = exponents[0].astype(jnp.float32).reshape(-1, 1)
    code_vals = jnp.clip(turned * jnp.exp2(expo_float), -code_limit, code_limit).astype(
        jnp.bfloat16
    )
    down_scale = jnp.exp2(-expo_float).astype(jnp.bfloat16)
    replicas = lax.axis_size("rep")
    own_rows = shard_rows // replicas
    got_codes = lax.all_to_all(
        code_vals.reshape(replicas, own_rows, head_count, head_size),
        "rep",
        split_axis=0,
        concat_axis=0,
        tiled=True,
    )
    got_scale = lax.all_to_all(
        down_scale.reshape(replicas, own_rows, head_count),
        "rep",
        split_axis=0,
        concat_axis=0,
        tiled=True,
    )
    unrotated = jnp.dot(
        got_codes.reshape(-1, head_size), sign_low, preferred_element_type=jnp.float32
    )
    unrotated = unrotated.reshape(got_codes.shape)
    summed = jnp.sum(unrotated * got_scale.astype(jnp.float32)[..., None], axis=0) * unit_scale
    mean_delta = summed.reshape(own_rows, columns) / replicas
    row_start = lax.axis_index("rep") * own_rows
    own_global = lax.dynamic_slice_in_dim(global_weight, row_start, own_rows, 0)
    new_momentum = momentum_decay * momentum.reshape(own_rows, columns) + mean_delta
    own_new = own_global - outer_rate * (mean_delta + momentum_decay * new_momentum)
    new_global = lax.all_gather(own_new, "rep", axis=0, tiled=True)
    return (new_global, new_momentum.reshape(1, 1, own_rows, columns))


def solution(mesh):
    placed = (
        P(("rep", "fsdp"), None),
        P(("rep", "fsdp"), None),
        P(),
        P("rep", "fsdp", None),
        P("rep", "fsdp", None),
        P("fsdp", None),
        P("fsdp", "rep", None, None),
    )
    return jax.shard_map(
        body,
        mesh=mesh,
        in_specs=placed,
        out_specs=(P("fsdp", None), P("fsdp", "rep", None, None)),
        check_vma=False,
    )
```

profile of v0, /device:TPU:1, one launch (start us, length us, event | category | flops | bytes accessed | tf_op | source)
XLA Modules:
  0.0 334.4 jit_solution(17300091209991733971)
XLA Ops:
  7.2 0.0 copy-start
  7.2 0.0 copy-start.1
  7.2 0.0 reduce-scatter.2.cloned.1.call-start
  7.2 1.5 fusion.2
  8.7 0.0 copy-done
  8.7 0.0 copy-done.1
  8.7 5.3 %convolution_convert_fusion = bf16[3072,1024]{1,0:T(8,128)(2,1)} fusion(bf16[128,1024]{1,0:T(8,128)(2,1)S(1)} %copy-done, bf16[128,3072]{1,0:T(8,128)(2,1)S(1)} %copy-done.1, f32[3072]{0:T(1024)} %param.9, f32[128]{0:T(128)S(1)} %add_rsqrt_fusion), kind=kOutput, calls=%fused_computation | convolution fusion | flops 810024960 | bytes 7352832 | tf_op jit(solution)/shard_map/dot_general | solution.py:33
  14.0 0.0 copy-start.4
  14.0 0.0 reduce-scatter.2.cloned.1.call-update
  14.0 0.7 copy-done.4
  14.7 0.1 copy.17
  14.8 0.7 exp2.38
  15.5 23.7 %all-to-all-start.1 = ((bf16[64,3,8]{2,1,0:T(4,128)(2,1)}), bf16[64,3,8]{2,1,0:T(4,128)(2,1)S(1)}, u32[]{:S(2)}, u32[]{:S(2)}) async-start(bf16[64,3,8]{2,1,0:T(4,128)(2,1)} %exp2.38), calls=%async_computation.2 | async-start | bytes 131072 | tf_op jit(solution)/shard_map/all_to_all | solution.py:62
  39.2 0.1 copy.16
  39.3 134.3 %reduce-scatter.2.cloned.1.call-done = bf16[192,1024]{1,0:T(8,128)(2,1)} async-done(((bf16[3072,1024]{1,0:T(8,128)(2,1)}), bf16[192,1024]{1,0:T(8,128)(2,1)}) %reduce-scatter.2.cloned.1.call-update) | async-done | bytes 393232 | tf_op jit(solution)/shard_map/reduce_scatter | solution.py:32
  173.6 1.8 fusion.6
  175.4 0.1 mul.86
  175.5 25.8 %psum.7 = f32[]{:T(128)} all-reduce(f32[]{:T(128)} %fusion.6), channel_id=1, replica_groups=mesh['rep'=64,'fsdp'=16] {'fsdp'}, use_global_device_ids=true, to_apply=%region_3.0 | all-reduce | flops 1 | bytes 8 | tf_op jit(solution)/shard_map/psum | solution.py:40
  202.0 0.0 copy-done.2
  202.0 1.1 fusion.7
  203.1 0.1 reshape.147
  203.3 1.7 fusion.1
  205.0 0.0 all-to-all-done.1
  205.0 21.1 %all-to-all-start = ((bf16[64,3,8,128]{3,2,1,0:T(8,128)(2,1)}), bf16[64,3,8,128]{3,2,1,0:T(8,128)(2,1)S(1)}, u32[]{:S(2)}, u32[]{:S(2)}) async-start(bf16[64,3,8,128]{3,2,1,0:T(8,128)(2,1)} %bitcast.1), calls=%async_computation.1 | async-start | bytes 786432 | tf_op jit(solution)/shard_map/all_to_all | solution.py:55
  226.0 0.0 copy-start.3
  226.1 16.3 %all-to-all-done = bf16[64,3,8,128]{3,2,1,0:T(8,128)(2,1)S(1)} async-done(((bf16[64,3,8,128]{3,2,1,0:T(8,128)(2,1)}), bf16[64,3,8,128]{3,2,1,0:T(8,128)(2,1)S(1)}, u32[]{:S(2)}, u32[]{:S(2)}) %all-to-all-start) | async-done | bytes 393248 | tf_op jit(solution)/shard_map/all_to_all | solution.py:55
  242.4 0.5 fusion.5
  242.9 0.0 copy-done.3
  242.9 0.9 fusion.23
  243.8 81.9 %all-gather = f32[64,3,1024]{2,1,0:T(4,128)S(1)} all-gather(f32[1,3,1024]{2,1,0:T(4,128)S(1)} %fusion.23), channel_id=1, replica_groups=mesh['rep'=64,'fsdp'=16] {'rep'}, dimensions={0}, use_global_device_ids=true | all-gather | bytes 798720 | tf_op jit(solution)/shard_map/all_gather | solution.py:79
  325.6 1.3 reshape.150
  326.9 0.6 copy.19
  (11 shorter events, 0.1 us)
Async XLA Ops:
  7.2 1.5 copy-start
  7.2 1.5 copy-start.1
  7.2 166.4 %reduce-scatter.2.cloned.1.call-start = ((), (), s32[]{:S(2)}) async-start(), calls=%async_computation.3 | async-start | bytes 6684672 | tf_op jit(solution)/shard_map/reduce_scatter | solution.py:32
  14.0 0.7 copy-start.4
  14.0 188.0 %copy-start.2 = (f32[1,192,1024]{2,1,0:T(8,128)S(1)}, f32[1,192,1024]{2,1,0:T(8,128)}, u32[]{:S(2)}) copy-start(f32[1,192,1024]{2,1,0:T(8,128)} %param.10) | copy-start | bytes 2359300
  15.5 189.4 %all-to-all-start.1 = ((bf16[64,3,8]{2,1,0:T(4,128)(2,1)}), bf16[64,3,8]{2,1,0:T(4,128)(2,1)S(1)}, u32[]{:S(2)}, u32[]{:S(2)}) async-start(bf16[64,3,8]{2,1,0:T(4,128)(2,1)} %exp2.38), calls=%async_computation.2 | async-start | bytes 131072 | tf_op jit(solution)/shard_map/all_to_all | solution.py:62
  205.0 37.4 %all-to-all-start = ((bf16[64,3,8,128]{3,2,1,0:T(8,128)(2,1)}), bf16[64,3,8,128]{3,2,1,0:T(8,128)(2,1)S(1)}, u32[]{:S(2)}, u32[]{:S(2)}) async-start(bf16[64,3,8,128]{3,2,1,0:T(8,128)(2,1)} %bitcast.1), calls=%async_computation.1 | async-start | bytes 786432 | tf_op jit(solution)/shard_map/all_to_all | solution.py:55
  226.0 16.8 %copy-start.3 = (f32[1,1,3,1024]{3,1,2,0:T(1,128)S(1)}, f32[1,1,3,1024]{3,1,2,0:T(1,128)}, u32[]{:S(2)}) copy-start(f32[1,1,3,1024]{3,1,2,0:T(1,128)} %param.13) | copy-start | bytes 36868
Sparse Core Ops, SparseCore 0:
  14.1 159.4 reduce-scatter.1
where the time goes:
time: 335 us; the launch traced here: 334 us
  waiting for transfers between devices  151 us (45%)
  blocking collectives  108 us (32%)
  starting transfers between devices  44.7 us (13%)
  between operations  14.9 us (4%)
  matrix products  7.45 us (2%)
  other arithmetic  5.3 us (2%)
  local copies, waits for them, and re-layouts  3.73 us (1%)
    reduce_scatter x1, waiting for transfers between devices, body(): lax.psum_scatter(lax.dot_general(normed, cotangent, (((0,), (0,)), ((), (...  134 us
    all_gather x1, blocking collectives, body(): new_global = lax.all_gather(own_new, 'rep', axis=0, tiled=True)  81.9 us
    psum x1, blocking collectives, body(): square = lax.psum(jnp.sum(gradient * gradient), 'fsdp')  25.8 us
    all_to_all x1, starting transfers between devices, body(): lax.all_to_all(down_scale.reshape(replicas, own_rows, head_count), 'rep',...  23.7 us
    all_to_all x1, starting transfers between devices, body(): lax.all_to_all(code_vals.reshape(replicas, own_rows, head_count, head_siz...  21.1 us
    all_to_all x1, waiting for transfers between devices, body(): lax.all_to_all(code_vals.reshape(replicas, own_rows, head_count, head_siz...  16.3 us
  transfers between devices with their start and end apart: 3, of which 2 were waited for; matrix products, arithmetic and copies ran while one was open for 2% of the time, Pallas kernels for 0%

commit v1 on v0

v1 whole, which is shorter than its diff:
```python
import functools

import jax
import jax.numpy as jnp
from jax import lax
from jax.experimental import pallas as pl
from jax.experimental.pallas import tpu as pltpu
from jax.sharding import PartitionSpec as P

inner_rate = 0.5
outer_rate = 0.7
momentum_decay = 0.9
code_limit = 7.0

BF16, F32 = jnp.bfloat16, jnp.float32
D, C, KVH, HD, TOK = 3072, 1024, 8, 128, 128
NXH, NZ, NCORE = 4, 8, 2
NY, NX = 8, 2
N_REP, N_FSDP, CHIPS = NXH * NZ * NCORE, NY * NX, NXH * NZ
ROWS = D // N_FSDP
OWN = ROWS // N_REP
BLK = OWN * KVH
FAR = NY // 2
PARTS = 4
HALF = PARTS // 2
CW = C // PARTS
GROUPS = 2 * FAR - 1
UNIT = HD ** (-0.5)


def hadamard():
    i = lax.broadcasted_iota(jnp.int32, (HD, HD), 0)
    j = lax.broadcasted_iota(jnp.int32, (HD, HD), 1)
    v = i & j
    for shift in (4, 2, 1):
        v = v ^ jnp.right_shift(v, shift)
    return jnp.where((v & 1) == 0, 1.0, -1.0).astype(BF16)


def rotate(v, signs):
    hi = v.astype(BF16)
    rest = v - hi.astype(F32)
    mid = rest.astype(BF16)
    low = (rest - mid.astype(F32)).astype(BF16)
    dot = functools.partial(jnp.dot, preferred_element_type=F32)
    return dot(hi, signs) + (dot(mid, signs) + dot(low, signs))


def kernel(tok, cot, gain, drift, expo, mom, upd_out, delta_out,
           nt, lhs, cot2, y_out, y_in, grad, base, limit, squares, codes, code_out, code_in, own_sum, sib_sum, upd,
           x_ss, x_rs, y_ss, y_rs, q_ss, q_rs, c_ss, c_rs, s_ss, s_rs, a_ss, a_rs, b_ss, b_rs, h_ss, h_rs):
    rep, f = lax.axis_index("rep"), lax.axis_index("fsdp")
    core = lax.rem(rep, NCORE)
    chip = rep // NCORE
    z, xh = lax.rem(chip, NZ), chip // NZ
    y, x = f // NX, lax.rem(f, NX)

    def rep_of(xh_, z_, core_):
        return (xh_ * NZ + z_) * NCORE + core_

    def at(rep_, f_):
        return {"rep": rep_, "fsdp": f_}

    def remote(src, dst, ss, rs, device):
        return pltpu.make_async_remote_copy(src_ref=src, dst_ref=dst, send_sem=ss, recv_sem=rs, device_id=device,
                                            device_id_type=pl.DeviceIdType.MESH)

    barrier = pltpu.get_barrier_semaphore()

    def greet_f(i, carry):
        pl.semaphore_signal(barrier, inc=1, device_id=at(rep, lax.rem(f + i, N_FSDP)), device_id_type=pl.DeviceIdType.MESH)
        return carry

    def greet_r(i, carry):
        pl.semaphore_signal(barrier, inc=1, device_id=at(lax.rem(rep + NCORE * i, N_REP), f),
                            device_id_type=pl.DeviceIdType.MESH)
        return carry

    lax.fori_loop(1, N_FSDP, greet_f, 0)
    lax.fori_loop(1, CHIPS, greet_r, 0)
    sibling = at(rep_of(xh, z, 1 - core), f)
    pl.semaphore_signal(barrier, inc=1, device_id=sibling, device_id_type=pl.DeviceIdType.MESH)

    wide = tok[...].astype(F32)
    scale = lax.rsqrt(jnp.mean(wide * wide, axis=-1, keepdims=True) + 1e-06)
    for b in range(D // HD):
        cols = slice(b * HD, (b + 1) * HD)
        block = tok[:, cols].astype(F32) * scale * gain[:, cols]
        nt[cols, :] = block.T.astype(BF16)

    pl.semaphore_wait(barrier, N_FSDP - 1 + CHIPS - 1 + 1)

    partner = at(rep, f + 1 - 2 * x)

    def cot_copy(p):
        return remote(cot.at[:, p * CW:(p + 1) * CW], cot2.at[p, TOK:, :], x_ss.at[p], x_rs.at[p], partner)

    def nt_rows(yy, xx):
        return pl.ds(pl.multiple_of((yy * NX + xx) * ROWS, ROWS), ROWS)

    def nt_copy(yy):
        return remote(nt.at[nt_rows(yy, 1 - x), :], lhs.at[yy, :, TOK:], x_ss.at[PARTS + yy], x_rs.at[PARTS + yy], partner)

    def dest(dist):
        return lax.rem(y + dist + NY, NY)

    order = [FAR] + [s * d for d in range(FAR - 1, 0, -1) for s in (1, -1)] + [0]
    sequence = [("c", 0), ("n", order[0]), ("c", HALF)]
    sequence += [("c", p) for p in range(PARTS) if p not in (0, HALF)]
    sequence += [("n", dist) for dist in order[1:]]
    for kind, which in sequence:
        (cot_copy(which) if kind == "c" else nt_copy(dest(which))).start()

    for p in range(PARTS):
        cot2[p, :TOK, :] = cot[:, p * CW:(p + 1) * CW]
    for yy in range(NY):
        lhs[yy, :, :TOK] = nt[nt_rows(yy, x), :]

    signs = hadamard()

    def y_copy(way, g, pp):
        return remote(y_out.at[way, g, pp], y_in.at[way, g, pp], y_ss.at[way, g, pp], y_rs.at[way, g, pp],
                      at(rep, dest(1 - 2 * way) * NX + x))

    def part_of(way, g, pp):
        return lax.rem(g + way, 2) * HALF + pp

    def partial_sum(yy, p):
        return jnp.dot(lhs[yy], cot2[p], preferred_element_type=F32)

    def y_send(g, ways, pps, ready):
        dist = FAR - (g + 1) // 2
        for pp in pps:
            for way in ways:
                value = partial_sum(dest((1 - 2 * way) * dist), part_of(way, g, pp))
                if ready:
                    y_copy(way, g - 2, pp).wait_recv()
                    value = value + y_in[way, g - 2, pp].astype(F32)
                y_out[way, g, pp] = value.astype(BF16)
                y_copy(way, g, pp).start()

    nt_copy(dest(FAR)).wait_recv()
    for pp in range(HALF):
        for way in range(2):
            cot_copy(way * HALF + pp).wait_recv()
            y_send(0, (way,), (pp,), False)
    for way in range(2):
        nt_copy(dest((1 - 2 * way) * (FAR - 1))).wait_recv()
    y_send(1, (0, 1), range(HALF), False)

    for k in range(KVH):
        cols = slice(k * HD, (k + 1) * HD)
        base[:, cols] = rotate(drift[0, :, cols], signs) * UNIT
        e = expo[0, :, k:k + 1].astype(F32)
        limit[:, cols] = jnp.broadcast_to(code_limit * jnp.exp2(-e), (ROWS, HD))

    y_send(2, (0, 1), range(HALF), True)
    for dist in order[3:]:
        nt_copy(dest(dist)).wait_recv()

    def y_step(g, carry):
        y_send(g, (0, 1), range(HALF), True)
        return carry

    lax.fori_loop(3, GROUPS, y_step, 0)

    total = jnp.zeros((8, CW), F32)
    for p in range(PARTS):
        value = partial_sum(y, p)
        for way in range(2):
            g = GROUPS - 1 if p // HALF == way else GROUPS - 2
            y_copy(way, g, p % HALF).wait_recv()
            value = value + y_in[way, g, p % HALF].astype(F32)
        grad[:, p * CW:(p + 1) * CW] = value
        total = total + jnp.sum((value * value).reshape(ROWS // 8, 8, CW), axis=0)
    mine = total[:, :HD]
    for i in range(1, CW // HD):
        mine = mine + total[:, i * HD:(i + 1) * HD]
    squares[f] = mine

    def q_copy(slot, ff):
        return remote(squares.at[slot], squares.at[slot], q_ss.at[ff], q_rs.at[slot], at(rep, ff))

    def q_start(i, carry):
        ff = lax.rem(f + i, N_FSDP)
        q_copy(f, ff).start()
        return carry

    lax.fori_loop(1, N_FSDP, q_start, 0)
    for k in range(KVH):
        cols = slice(k * HD, (k + 1) * HD)
        grad[:, cols] = rotate(grad[:, cols], signs) * (UNIT * inner_rate)

    def q_wait(i, carry):
        q_copy(lax.rem(f + i, N_FSDP), lax.rem(f + i, N_FSDP)).wait_recv()
        return carry

    lax.fori_loop(1, N_FSDP, q_wait, 0)
    square = jnp.sum(jnp.sum(squares[...], axis=0), keepdims=True)
    factor = jnp.minimum(1.0, 1.0 / jnp.sqrt(square * (1.0 / (D * C)) + 1e-06))

    for k in range(KVH):
        cols = slice(k * HD, (k + 1) * HD)
        bound = limit[:, cols]
        value = base[:, cols] + factor * grad[:, cols]
        codes[pl.ds(k, ROWS, stride=KVH), :] = jnp.clip(value, -bound, bound)
    code_out[...] = codes[...].reshape(CHIPS, NCORE * BLK, HD).astype(BF16)

    def c_copy(src, slot, there):
        return remote(code_out.at[src], code_in.at[slot], c_ss.at[src], c_rs.at[slot], at(there * NCORE + core, f))

    def other(i):
        return lax.rem(xh + i // NZ, NXH) * NZ + lax.rem(z + i, NZ)

    def c_start(i, carry):
        there = other(i)
        c_copy(there, chip, there).start()
        return carry

    lax.fori_loop(1, CHIPS, c_start, 0)
    code_in[chip] = code_out[chip]

    rows = [(j, k) for j in range(OWN) for k in range(KVH)]
    moved = jnp.concatenate([mom[0, 0, j:j + 1, k * HD:(k + 1) * HD] for j, k in rows], axis=0)

    def c_wait(i, carry):
        there = other(i)
        c_copy(there, there, there).wait_recv()
        return carry

    lax.fori_loop(1, CHIPS, c_wait, 0)
    summed = jnp.sum(code_in[...].astype(F32), axis=0)
    for c in range(NCORE):
        own_sum[c] = summed[c * BLK:(c + 1) * BLK]
    sib_copy = remote(own_sum.at[1 - core], sib_sum, s_ss.at[0], s_rs.at[0], sibling)
    sib_copy.start()
    sib_copy.wait_recv()
    mean_delta = rotate(own_sum[core] + sib_sum[...], signs) * (UNIT / N_REP)
    new_momentum = momentum_decay * moved + mean_delta
    upd[xh, z, core] = outer_rate * (mean_delta + momentum_decay * new_momentum)

    def a_copy(i, slot_z, slot_x, there_z, there_x, sem):
        return remote(upd.at[slot_x, slot_z, core], upd.at[slot_x, slot_z, core], a_ss.at[i], a_rs.at[sem],
                      at(rep_of(there_x, there_z, core), f))

    @pl.when(core == 0)
    def _():
        for i in range(1, NZ):
            a_copy(i, z, xh, lax.rem(z + i, NZ), xh, z).start()
        for i in range(1, NZ):
            zz = lax.rem(z + i, NZ)
            a_copy(i, zz, xh, zz, xh, zz).wait_recv()

        def line(i, row, there, sem):
            return remote(upd.at[row, :, 0], upd.at[row, :, 0], b_ss.at[i], b_rs.at[sem], at(rep_of(there, z, 0), f))

        def hand(row):
            return remote(upd.at[row, :, 0], upd.at[row, :, 0], h_ss.at[row], h_rs.at[row], sibling)

        for i in range(1, NXH):
            line(i, xh, lax.rem(xh + i, NXH), xh).start()
        hand(xh).start()
        for i in range(1, NXH):
            xx = lax.rem(xh + i, NXH)
            line(i, xx, xx, xx).wait_recv()
            hand(xx).start()
        for r in range(NZ):
            remote(upd.at[:, r, 1], upd.at[:, r, 1], h_ss.at[r], h_rs.at[r], sibling).wait_recv()
        for r in range(NXH):
            hand(r).wait_send()
        for i in range(1, NXH):
            line(i, xh, xh, xh).wait_send()
        for i in range(1, NZ):
            a_copy(i, z, xh, z, xh, z).wait_send()

    @pl.when(core == 1)
    def _():
        for i in range(1, NXH):
            a_copy(i, z, xh, z, lax.rem(xh + i, NXH), xh).start()
        for i in range(1, NXH):
            xx = lax.rem(xh + i, NXH)
            a_copy(i, z, xx, z, xx, xx).wait_recv()

        def line(i, row, there, sem):
            return remote(upd.at[:, row, 1], upd.at[:, row, 1], b_ss.at[i], b_rs.at[sem], at(rep_of(xh, there, 1), f))

        def hand(row):
            return remote(upd.at[:, row, 1], upd.at[:, row, 1], h_ss.at[row], h_rs.at[row], sibling)

        for i in range(1, NZ):
            line(i, z, lax.rem(z + i, NZ), z).start()
        hand(z).start()
        for i in range(1, NZ):
            zz = lax.rem(z + i, NZ)
            line(i, zz, zz, zz).wait_recv()
            hand(zz).start()
        for r in range(NXH):
            remote(upd.at[r, :, 0], upd.at[r, :, 0], h_ss.at[r], h_rs.at[r], sibling).wait_recv()
        for r in range(NZ):
            hand(r).wait_send()
        for i in range(1, NZ):
            line(i, z, z, z).wait_send()
        for i in range(1, NXH):
            a_copy(i, z, xh, z, xh, xh).wait_send()

    flat = upd.reshape(ROWS * KVH, HD)
    for k in range(KVH):
        upd_out[:, k * HD:(k + 1) * HD] = flat[pl.ds(k, ROWS, stride=KVH), :]
    for i, (j, k) in enumerate(rows):
        delta_out[j:j + 1, k * HD:(k + 1) * HD] = mean_delta[i:i + 1, :]

    for p in range(PARTS):
        cot_copy(p).wait_send()
    for yy in range(NY):
        nt_copy(yy).wait_send()

    def y_drain(g, carry):
        for way in range(2):
            for pp in range(HALF):
                y_copy(way, g, pp).wait_send()
        return carry

    lax.fori_loop(0, GROUPS, y_drain, 0)

    def q_drain(i, carry):
        q_copy(f, lax.rem(f + i, N_FSDP)).wait_send()
        return carry

    lax.fori_loop(1, N_FSDP, q_drain, 0)

    def c_drain(i, carry):
        there = other(i)
        c_copy(there, chip, there).wait_send()
        return carry

    lax.fori_loop(1, CHIPS, c_drain, 0)
    sib_copy.wait_send()


def body(tokens, cotangent, norm_gain, replica_drift, exponents, global_weight, momentum):
    dma = pltpu.SemaphoreType.DMA
    vmem = pl.BlockSpec(memory_space=pltpu.VMEM)
    update, mean_delta = pl.pallas_call(
        kernel,
        out_shape=(jax.ShapeDtypeStruct((ROWS, C), F32), jax.ShapeDtypeStruct((OWN, C), F32)),
        in_specs=[vmem] * 6,
        out_specs=(vmem, vmem),
        scratch_shapes=[
            pltpu.VMEM((D, TOK), BF16),
            pltpu.VMEM((NY, ROWS, NX * TOK), BF16),
            pltpu.VMEM((PARTS, NX * TOK, CW), BF16),
            pltpu.VMEM((2, GROUPS, HALF, ROWS, CW), BF16),
            pltpu.VMEM((2, GROUPS, HALF, ROWS, CW), BF16),
            pltpu.VMEM((ROWS, C), F32),
            pltpu.VMEM((ROWS, C), F32),
            pltpu.VMEM((ROWS, C), F32),
            pltpu.VMEM((N_FSDP, 8, HD), F32),
            pltpu.VMEM((ROWS * KVH, HD), F32),
            pltpu.VMEM((CHIPS, NCORE * BLK, HD), BF16),
            pltpu.VMEM((CHIPS, NCORE * BLK, HD), BF16),
            pltpu.VMEM((NCORE, BLK, HD), F32),
            pltpu.VMEM((BLK, HD), F32),
            pltpu.VMEM((NXH, NZ, NCORE, BLK, HD), F32),
            dma((PARTS + NY,)), dma((PARTS + NY,)),
            dma((2, GROUPS, HALF)), dma((2, GROUPS, HALF)),
            dma((N_FSDP,)), dma((N_FSDP,)),
            dma((CHIPS,)), dma((CHIPS,)),
            dma((1,)), dma((1,)),
            dma((NZ,)), dma((NZ,)),
            dma((NZ,)), dma((NZ,)),
            dma((NZ,)), dma((NZ,)),
        ],
        compiler_params=pltpu.CompilerParams(collective_id=0, has_side_effects=True, vmem_limit_bytes=48 * 1024 * 1024),
        cost_estimate=pl.CostEstimate(flops=2 * TOK * D * C, bytes_accessed=4 * 1024 * 1024, transcendentals=0),
    )(tokens, cotangent, norm_gain.reshape(1, D), replica_drift, exponents, momentum)
    new_global = global_weight - update
    new_momentum = momentum_decay * momentum + mean_delta.reshape(momentum.shape)
    return new_global, new_momentum


def solution(mesh):
    placed = (
        P(("rep", "fsdp"), None),
        P(("rep", "fsdp"), None),
        P(),
        P("rep", "fsdp", None),
        P("rep", "fsdp", None),
        P("fsdp", None),
        P("fsdp", "rep", None, None),
    )
    return jax.shard_map(
        body,
        mesh=mesh,
        in_specs=placed,
        out_specs=(P("fsdp", None), P("fsdp", "rep", None, None)),
        check_vma=False,
    )
```

time: 335 us -> 105 us (0.31)
  waiting for transfers between devices: 151 us -> 0 us
  blocking collectives: 108 us -> 0 us
  Pallas kernels: 0 us -> 97.7 us
  starting transfers between devices: 44.7 us -> 0 us
  between operations: 14.9 us -> 0.68 us
  matrix products: 7.45 us -> 0 us
  other arithmetic: 5.3 us -> 1 us
    reduce_scatter x1 -> x0, waiting for transfers between devices: 134 us -> none  [body(): lax.psum_scatter(lax.dot_general(normed, cotangent, (((0,), (0,)), ((), (...]
    pallas_call x0 -> x1, Pallas kernels: none -> 97.7 us  [body(): pl.pallas_call(kernel, out_shape=(jax.ShapeDtypeStruct((ROWS, C), F32), j...]
    all_gather x1 -> x0, blocking collectives: 81.9 us -> none  [body(): new_global = lax.all_gather(own_new, 'rep', axis=0, tiled=True)]
    all_to_all x2 -> x0, starting transfers between devices: 44.7 us -> none  [the longest x1 23.7 us: body(): lax.all_to_all(down_scale.reshape(replicas, own_rows, head_count), 'rep',...]
    psum x1 -> x0, blocking collectives: 25.8 us -> none  [body(): square = lax.psum(jnp.sum(gradient * gradient), 'fsdp')]
    all_to_all x2 -> x0, waiting for transfers between devices: 16.3 us -> none  [the longest x1 16.3 us: body(): lax.all_to_all(code_vals.reshape(replicas, own_rows, head_count, head_siz...]
    dot_general x3 -> x0, matrix products: 7.45 us -> none  [the longest x1 5.27 us: body(): lax.dot_general(normed, cotangent, (((0,), (0,)), ((), ())), preferred_el...]
  transfers between devices with their start and end apart: 3 -> 0, of which waited for: 2 -> 0; matrix products, arithmetic and copies ran while one was open for 2% -> 0% of each run, Pallas kernels for 0% -> 0%
where the time goes in v1:
time: 105 us
  Pallas kernels  97.7 us (93%)
  local copies, waits for them, and re-layouts  5.26 us (5%)
    pallas_call x1, Pallas kernels, body(): pl.pallas_call(kernel, out_shape=(jax.ShapeDtypeStruct((ROWS, C), F32), j...  97.7 us
    unnamed x17, local copies, waits for them, and re-layouts  5.26 us

profile of v1, /device:TPU:1, one launch (start us, length us, event | category | flops | bytes accessed | tf_op | source)
XLA Modules:
  0.0 104.6 jit_solution(9037153515756419648)
XLA Ops:
  0.6 0.0 copy-start.6
  0.6 0.7 copy.10.mom
  1.4 0.0 copy-done.6
  1.4 0.0 copy-start.3
  1.4 0.1 copy.9.expo
  1.5 0.6 copy-done.3
  2.1 0.0 copy-start
  2.1 1.1 %copy-done = bf16[128,3072]{1,0:T(8,128)(2,1)S(1)} copy-done((bf16[128,3072]{1,0:T(8,128)(2,1)S(1)}, bf16[128,3072]{1,0:T(8,128)(2,1)}, u32[]{:S(2)}) %copy-start) | copy-done | bytes 786456
  3.2 0.0 copy-start.1
  3.2 1.1 %copy-done.1 = f32[1,192,1024]{2,1,0:T(8,128)S(1)} copy-done((f32[1,192,1024]{2,1,0:T(8,128)S(1)}, f32[1,192,1024]{2,1,0:T(8,128)}, u32[]{:S(2)}) %copy-start.1) | copy-done | bytes 786456
  4.3 0.0 copy-start.2
  4.3 0.9 copy-done.2
  5.3 0.0 copy-start.4
  5.3 97.7 %shard_map.86 = (f32[192,1024]{1,0:T(8,128)S(1)}, f32[3,1024]{1,0:T(4,128)S(1)}) custom-call(bf16[128,3072]{1,0:T(8,128)(2,1)S(1)} %copy-done, bf16[128,1024]{1,0:T(8,128)(2,1)S(1)} %copy-done.2, f32[1,3072]{1,0:T(1,128)S(1)} %bitcast.3, f32[1,192,1024]{2,1,0:T(8,128)S(1)} %copy-done.1, s32[1,192,8]{2,1,0:T(8,128)S(1)} %copy.9.expo, ...), custom_call_target="tpu_custom_call" | custom-call | flops 805306368 | bytes 4194304 | tf_op jit(solution)/shard_map/pallas_call | solution.py:343
  103.0 0.0 copy-done.4
  103.0 0.0 copy-start.5
  103.0 1.0 sub.3
  104.0 0.0 copy-done.5
  104.0 0.6 copy.12
  (1 shorter events, 0.0 us)
Async XLA Ops:
  0.6 0.7 copy-start.6
  1.4 0.7 copy-start.3
  2.1 1.1 %copy-start = (bf16[128,3072]{1,0:T(8,128)(2,1)S(1)}, bf16[128,3072]{1,0:T(8,128)(2,1)}, u32[]{:S(2)}) copy-start(bf16[128,3072]{1,0:T(8,128)(2,1)} %tok.1) | copy-start | bytes 2359300
  3.2 1.1 %copy-start.1 = (f32[1,192,1024]{2,1,0:T(8,128)S(1)}, f32[1,192,1024]{2,1,0:T(8,128)}, u32[]{:S(2)}) copy-start(f32[1,192,1024]{2,1,0:T(8,128)} %drift.1) | copy-start | bytes 2359300
  4.3 0.9 copy-start.2
  5.3 97.7 %copy-start.4 = (f32[192,1024]{1,0:T(8,128)S(1)}, f32[192,1024]{1,0:T(8,128)}, u32[]{:S(2)}) copy-start(f32[192,1024]{1,0:T(8,128)} %param.12) | copy-start | bytes 2359300
  103.0 1.0 copy-start.5

commit v2 on v1

v2 whole, which is shorter than its diff:
```python
import functools

import jax
import jax.numpy as jnp
from jax import lax
from jax.experimental import pallas as pl
from jax.experimental.pallas import tpu as pltpu
from jax.sharding import PartitionSpec as P

inner_rate = 0.5
outer_rate = 0.7
momentum_decay = 0.9
code_limit = 7.0

BF16, F32 = jnp.bfloat16, jnp.float32
D, C, KVH, HD, TOK = 3072, 1024, 8, 128, 128
NXH, NZ, NCORE = 4, 8, 2
NY, NX = 8, 2
N_REP, N_FSDP, CHIPS = NXH * NZ * NCORE, NY * NX, NXH * NZ
ROWS = D // N_FSDP
OWN = ROWS // N_REP
BLK = OWN * KVH
FAR = NY // 2
PARTS = 4
HALF = ROWS // 2
CW = C // PARTS
GROUPS = 2 * FAR - 1
UNIT = HD ** (-0.5)
ENCODE_MIB, COMBINE_MIB = 60, 60


def hadamard():
    i = lax.broadcasted_iota(jnp.int32, (HD, HD), 0)
    j = lax.broadcasted_iota(jnp.int32, (HD, HD), 1)
    v = i & j
    for shift in (4, 2, 1):
        v = v ^ jnp.right_shift(v, shift)
    return jnp.where((v & 1) == 0, 1.0, -1.0).astype(BF16)


def split(v):
    hi = v.astype(BF16)
    rest = v - hi.astype(F32)
    mid = rest.astype(BF16)
    return hi, mid, (rest - mid.astype(F32)).astype(BF16)


def rotate(v, signs, terms):
    parts = split(v)[:terms]
    return jnp.dot(jnp.concatenate(parts, axis=1), jnp.concatenate([signs] * terms, axis=0), preferred_element_type=F32)


def place():
    rep, f = lax.axis_index("rep"), lax.axis_index("fsdp")
    chip = rep // NCORE
    return rep, f, lax.rem(rep, NCORE), chip, lax.rem(chip, NZ), chip // NZ


def at(rep, f):
    return {"rep": rep, "fsdp": f}


def remote(src, dst, ss, rs, device):
    return pltpu.make_async_remote_copy(src_ref=src, dst_ref=dst, send_sem=ss, recv_sem=rs, device_id=device,
                                        device_id_type=pl.DeviceIdType.MESH)


def greet(barrier, device):
    pl.semaphore_signal(barrier, inc=1, device_id=device, device_id_type=pl.DeviceIdType.MESH)


def encode(tok_hbm, cot, gain_hbm, drift_hbm, expo_hbm, code_out,
           tok, gain, drift, expo, l_s, nt, lhs, cot2, y_out, y_in, grad, base, limit, squares, codes,
           x_ss, x_rs, y_ss, y_rs, q_ss, q_rs):
    rep, f, _, _, _, _ = place()
    y, x = f // NX, lax.rem(f, NX)

    def cot_load(p):
        return pltpu.make_async_copy(cot.at[:, p * CW:(p + 1) * CW], cot2.at[p, :TOK, :], l_s.at[p])

    loads = [pltpu.make_async_copy(src, dst, l_s.at[PARTS + i]) for i, (src, dst) in enumerate(
        ((tok_hbm, tok), (gain_hbm, gain), (drift_hbm, drift), (expo_hbm, expo)))]
    loads[0].start()
    loads[1].start()
    for p in range(PARTS):
        cot_load(p).start()
    for load in loads[2:]:
        load.start()

    barrier = pltpu.get_barrier_semaphore()

    def greet_f(i, carry):
        greet(barrier, at(rep, lax.rem(f + i, N_FSDP)))
        return carry

    lax.fori_loop(1, N_FSDP, greet_f, 0)
    pl.semaphore_wait(barrier, N_FSDP - 1)

    partner = at(rep, f + 1 - 2 * x)

    def cot_copy(p):
        return remote(cot.at[:, p * CW:(p + 1) * CW], cot2.at[p, TOK:, :], x_ss.at[p], x_rs.at[p], partner)

    def nt_rows(yy, xx):
        return pl.ds(pl.multiple_of((yy * NX + xx) * ROWS, ROWS), ROWS)

    def nt_copy(yy):
        return remote(nt.at[nt_rows(yy, 1 - x), :], lhs.at[yy, :, TOK:], x_ss.at[PARTS + yy], x_rs.at[PARTS + yy], partner)

    def dest(dist):
        return lax.rem(y + dist + NY, NY)

    cot_copy(0).start()
    cot_copy(1).start()

    loads[0].wait()
    loads[1].wait()
    wide = tok[...].astype(F32)
    scale = lax.rsqrt(jnp.mean(wide * wide, axis=-1, keepdims=True) + 1e-06)

    def norm_chunk(dist):
        yy = dest(dist)
        for b in range(NX * ROWS // HD):
            cols = pl.ds(pl.multiple_of(yy * (NX * ROWS) + b * HD, HD), HD)
            block = tok[:, cols].astype(F32) * scale * gain[:, cols]
            nt[cols, :] = block.T.astype(BF16)
        nt_copy(yy).start()
        lhs[yy, :, :TOK] = nt[nt_rows(yy, x), :]

    norm_chunk(FAR)
    for p in range(2, PARTS):
        cot_copy(p).start()
    norm_chunk(FAR - 1)
    norm_chunk(1 - FAR)

    signs = hadamard()

    def y_copy(way, g, p):
        return remote(y_out.at[way, g, p], y_in.at[way, g, p], y_ss.at[way], y_rs.at[way, g, p],
                      at(rep, dest(1 - 2 * way) * NX + x))

    def half_of(way, g):
        return pl.ds(pl.multiple_of(lax.rem(g + way, 2) * HALF, HALF), HALF)

    def y_send(g, p, ready):
        dist = FAR - (g + 1) // 2
        rows = [lhs[dest((1 - 2 * way) * dist), half_of(way, g), :] for way in range(2)]
        both = jnp.dot(jnp.concatenate(rows, axis=0), cot2[p], preferred_element_type=F32)
        for way in range(2):
            value = both[way * HALF:(way + 1) * HALF]
            if ready:
                y_copy(way, g - 2, p).wait_recv()
                value = value + y_in[way, g - 2, p].astype(F32)
            y_out[way, g, p] = value.astype(BF16)
            y_copy(way, g, p).start()

    for p in range(PARTS):
        cot_load(p).wait()
    nt_copy(dest(FAR)).wait_recv()
    for p in range(PARTS):
        cot_copy(p).wait_recv()
        y_send(0, p, False)
    norm_chunk(FAR - 2)
    norm_chunk(2 - FAR)
    for way in range(2):
        nt_copy(dest((1 - 2 * way) * (FAR - 1))).wait_recv()
    for p in range(PARTS):
        y_send(1, p, False)
    rest = [0] + [s * d for d in range(1, FAR - 2) for s in (1, -1)]
    for dist in rest[1:] + rest[:1]:
        norm_chunk(dist)
    for p in range(PARTS):
        y_send(2, p, True)

    for load in loads[2:]:
        load.wait()
    for k in range(KVH):
        cols = slice(k * HD, (k + 1) * HD)
        base[:, cols] = rotate(drift[0, :, cols], signs, 2) * UNIT
    head = lax.broadcasted_iota(jnp.int32, (KVH, C), 0) == lax.broadcasted_iota(jnp.int32, (KVH, C), 1) // HD
    bounds = (code_limit * jnp.exp2(-expo[...].astype(F32))).astype(BF16)
    limit[...] = lax.dot_general(bounds, head.astype(BF16), (((0,), (0,)), ((), ())), preferred_element_type=F32)

    for dist in [FAR - 2, 2 - FAR] + rest:
        nt_copy(dest(dist)).wait_recv()

    def y_step(g, carry):
        for p in range(PARTS):
            y_send(g, p, True)
        return carry

    lax.fori_loop(3, GROUPS, y_step, 0)

    total = jnp.zeros((8, CW), F32)
    for p in range(PARTS):
        cols = slice(p * CW, (p + 1) * CW)
        value = jnp.dot(lhs[y], cot2[p], preferred_element_type=F32)
        for way in range(2):
            y_copy(way, GROUPS - 2, p).wait_recv()
        early = [y_in[1 - half, GROUPS - 2, p].astype(F32) for half in range(2)]
        for half in range(2):
            rows = slice(half * HALF, (half + 1) * HALF)
            y_copy(half, GROUPS - 1, p).wait_recv()
            some = value[rows] + early[half] + y_in[half, GROUPS - 1, p].astype(F32)
            grad[rows, cols] = some
            total = total + jnp.sum((some * some).reshape(HALF // 8, 8, CW), axis=0)
    mine = total[:, :HD]
    for i in range(1, CW // HD):
        mine = mine + total[:, i * HD:(i + 1) * HD]
    squares[f] = mine

    def q_start(i, carry):
        remote(squares.at[f], squares.at[f], q_ss.at[0], q_rs.at[0], at(rep, lax.rem(f + i, N_FSDP))).start()
        return carry

    lax.fori_loop(1, N_FSDP, q_start, 0)
    for k in range(KVH):
        cols = slice(k * HD, (k + 1) * HD)
        grad[:, cols] = rotate(grad[:, cols], signs, 2) * (UNIT * inner_rate)

    for p in range(PARTS):
        cot_copy(p).wait_send()
    for yy in range(NY):
        nt_copy(yy).wait_send()
    for way in range(2):
        remote(y_out.at[way], y_in.at[way], y_ss.at[way], y_rs.at[0, 0, 0], at(rep, dest(1 - 2 * way) * NX + x)).wait_send()
    others = pl.ds(0, N_FSDP - 1)
    all_squares = remote(squares.at[others], squares.at[others], q_ss.at[0], q_rs.at[0], at(rep, lax.rem(f + 1, N_FSDP)))
    all_squares.wait_send()
    all_squares.wait_recv()
    square = jnp.sum(jnp.sum(squares[...], axis=0), keepdims=True)
    factor = jnp.minimum(1.0, 1.0 / jnp.sqrt(square * (1.0 / (D * C)) + 1e-06))

    for k in range(KVH):
        cols = slice(k * HD, (k + 1) * HD)
        bound = limit[:, cols]
        codes[pl.ds(k, ROWS, stride=KVH), :] = jnp.clip(base[:, cols] + factor * grad[:, cols], -bound, bound)
    code_out[...] = codes[...].reshape(CHIPS, NCORE * BLK, HD).astype(BF16)


def combine(code_out, mom, upd_out, delta_out,
            code_in, own_sum, sib_sum, upd, c_ss, c_rs, s_ss, s_rs, a_ss, a_rs, b_ss, b_rs, h_ss, h_rs):
    rep, f, core, chip, z, xh = place()

    def rep_of(xh_, z_, core_):
        return (xh_ * NZ + z_) * NCORE + core_

    barrier = pltpu.get_barrier_semaphore()

    def greet_r(i, carry):
        greet(barrier, at(lax.rem(rep + NCORE * i, N_REP), f))
        return carry

    lax.fori_loop(1, CHIPS, greet_r, 0)
    sibling = at(rep_of(xh, z, 1 - core), f)
    greet(barrier, sibling)
    pl.semaphore_wait(barrier, CHIPS)

    def c_start(i, carry):
        there = lax.rem(xh + lax.rem(i // NZ + 2, NXH), NXH) * NZ + lax.rem(z + i, NZ)

        @pl.when(there != chip)
        def _():
            remote(code_out.at[there], code_in.at[chip], c_ss.at[0], c_rs.at[0], at(there * NCORE + core, f)).start()

        return carry

    lax.fori_loop(0, CHIPS, c_start, 0)
    own_code = pltpu.make_async_copy(code_out.at[chip], code_in.at[chip], s_ss.at[1])
    own_code.start()
    others = pl.ds(0, CHIPS - 1)
    all_codes = remote(code_out.at[others], code_in.at[others], c_ss.at[0], c_rs.at[0], sibling)
    own_code.wait()
    all_codes.wait_send()
    all_codes.wait_recv()
    summed = jnp.sum(code_in[...].astype(F32), axis=0)
    for c in range(NCORE):
        own_sum[c] = summed[c * BLK:(c + 1) * BLK]
    sib_copy = remote(own_sum.at[1 - core], sib_sum, s_ss.at[0], s_rs.at[0], sibling)
    sib_copy.start()
    sib_copy.wait()
    signs = hadamard()
    mean_delta = rotate(own_sum[core] + sib_sum[...], signs, 3) * (UNIT / N_REP)
    new_momentum = momentum_decay * mom[...] + mean_delta
    upd[xh, z, core] = outer_rate * (mean_delta + momentum_decay * new_momentum)

    def a_copy(i, slot_z, slot_x, there_z, there_x, sem):
        return remote(upd.at[slot_x, slot_z, core], upd.at[slot_x, slot_z, core], a_ss.at[i], a_rs.at[sem],
                      at(rep_of(there_x, there_z, core), f))

    @pl.when(core == 0)
    def _():
        for i in range(1, NZ):
            a_copy(i, z, xh, lax.rem(z + i, NZ), xh, z).start()
        for i in range(1, NZ):
            zz = lax.rem(z + i, NZ)
            a_copy(i, zz, xh, zz, xh, zz).wait_recv()

        def line(i, row, there, sem):
            return remote(upd.at[row, :, 0], upd.at[row, :, 0], b_ss.at[i], b_rs.at[sem], at(rep_of(there, z, 0), f))

        def hand(row):
            return remote(upd.at[row, :, 0], upd.at[row, :, 0], h_ss.at[row], h_rs.at[row], sibling)

        for i in range(1, NXH):
            line(i, xh, lax.rem(xh + i, NXH), xh).start()
        hand(xh).start()
        for i in range(1, NXH):
            xx = lax.rem(xh + i, NXH)
            line(i, xx, xx, xx).wait_recv()
            hand(xx).start()
        for r in range(NZ):
            remote(upd.at[:, r, 1], upd.at[:, r, 1], h_ss.at[r], h_rs.at[r], sibling).wait_recv()
        for r in range(NXH):
            hand(r).wait_send()
        for i in range(1, NXH):
            line(i, xh, xh, xh).wait_send()
        for i in range(1, NZ):
            a_copy(i, z, xh, z, xh, z).wait_send()

    @pl.when(core == 1)
    def _():
        for i in range(1, NXH):
            a_copy(i, z, xh, z, lax.rem(xh + i, NXH), xh).start()
        for i in range(1, NXH):
            xx = lax.rem(xh + i, NXH)
            a_copy(i, z, xx, z, xx, xx).wait_recv()

        def line(i, row, there, sem):
            return remote(upd.at[:, row, 1], upd.at[:, row, 1], b_ss.at[i], b_rs.at[sem], at(rep_of(xh, there, 1), f))

        def hand(row):
            return remote(upd.at[:, row, 1], upd.at[:, row, 1], h_ss.at[row], h_rs.at[row], sibling)

        for i in range(1, NZ):
            line(i, z, lax.rem(z + i, NZ), z).start()
        hand(z).start()
        for i in range(1, NZ):
            zz = lax.rem(z + i, NZ)
            line(i, zz, zz, zz).wait_recv()
            hand(zz).start()
        for r in range(NXH):
            remote(upd.at[r, :, 0], upd.at[r, :, 0], h_ss.at[r], h_rs.at[r], sibling).wait_recv()
        for r in range(NZ):
            hand(r).wait_send()
        for i in range(1, NZ):
            line(i, z, z, z).wait_send()
        for i in range(1, NXH):
            a_copy(i, z, xh, z, xh, xh).wait_send()

    flat = upd.reshape(ROWS * KVH, HD)
    for k in range(KVH):
        upd_out[:, k * HD:(k + 1) * HD] = flat[pl.ds(k, ROWS, stride=KVH), :]
    delta_out[...] = mean_delta


def body(tokens, cotangent, norm_gain, replica_drift, exponents, global_weight, momentum):
    dma = pltpu.SemaphoreType.DMA
    vmem = pl.BlockSpec(memory_space=pltpu.VMEM)
    hbm = pl.BlockSpec(memory_space=pl.ANY)
    own_rows = momentum.reshape(BLK, HD)
    codes = pl.pallas_call(
        encode,
        out_shape=jax.ShapeDtypeStruct((CHIPS, NCORE * BLK, HD), BF16),
        in_specs=[hbm] * 5,
        out_specs=vmem,
        scratch_shapes=[
            pltpu.VMEM((TOK, D), BF16),
            pltpu.VMEM((1, D), F32),
            pltpu.VMEM((1, ROWS, C), F32),
            pltpu.VMEM((KVH, ROWS), jnp.int32),
            dma((PARTS + 4,)),
            pltpu.VMEM((D, TOK), BF16),
            pltpu.VMEM((NY, ROWS, NX * TOK), BF16),
            pltpu.VMEM((PARTS, NX * TOK, CW), BF16),
            pltpu.VMEM((2, GROUPS, PARTS, HALF, CW), BF16),
            pltpu.VMEM((2, GROUPS, PARTS, HALF, CW), BF16),
            pltpu.VMEM((ROWS, C), F32),
            pltpu.VMEM((ROWS, C), F32),
            pltpu.VMEM((ROWS, C), F32),
            pltpu.VMEM((N_FSDP, 8, HD), F32),
            pltpu.VMEM((ROWS * KVH, HD), F32),
            dma((PARTS + NY,)), dma((PARTS + NY,)),
            dma((2,)), dma((2, GROUPS, PARTS)),
            dma((1,)), dma((1,)),
        ],
        compiler_params=pltpu.CompilerParams(collective_id=0, has_side_effects=True, vmem_limit_bytes=ENCODE_MIB * 2 ** 20),
        cost_estimate=pl.CostEstimate(flops=2 * TOK * D * C, bytes_accessed=4 * 1024 * 1024, transcendentals=0),
    )(tokens, cotangent, norm_gain.reshape(1, D), replica_drift, exponents[0].T)
    update, mean_delta = pl.pallas_call(
        combine,
        out_shape=(jax.ShapeDtypeStruct((ROWS, C), F32), jax.ShapeDtypeStruct((BLK, HD), F32)),
        in_specs=[hbm, vmem],
        out_specs=(vmem, vmem),
        scratch_shapes=[
            pltpu.VMEM((CHIPS, NCORE * BLK, HD), BF16),
            pltpu.VMEM((NCORE, BLK, HD), F32),
            pltpu.VMEM((BLK, HD), F32),
            pltpu.VMEM((NXH, NZ, NCORE, BLK, HD), F32),
            dma((1,)), dma((1,)),
            dma((2,)), dma((1,)),
            dma((NZ,)), dma((NZ,)),
            dma((NZ,)), dma((NZ,)),
            dma((NZ,)), dma((NZ,)),
        ],
        compiler_params=pltpu.CompilerParams(collective_id=1, has_side_effects=True, vmem_limit_bytes=COMBINE_MIB * 2 ** 20),
        cost_estimate=pl.CostEstimate(flops=2 * ROWS * C * HD, bytes_accessed=2 * 1024 * 1024, transcendentals=0),
    )(codes, own_rows)
    new_global = global_weight - update
    new_momentum = momentum_decay * own_rows + mean_delta
    return new_global, new_momentum.reshape(momentum.shape)


def solution(mesh):
    placed = (
        P(("rep", "fsdp"), None),
        P(("rep", "fsdp"), None),
        P(),
        P("rep", "fsdp", None),
        P("rep", "fsdp", None),
        P("fsdp", None),
        P("fsdp", "rep", None, None),
    )
    return jax.shard_map(
        body,
        mesh=mesh,
        in_specs=placed,
        out_specs=(P("fsdp", None), P("fsdp", "rep", None, None)),
        check_vma=False,
    )
```

time: 105 us -> 106 us (level)
  Pallas kernels: 97.7 us -> 103 us
  local copies, waits for them, and re-layouts: 5.26 us -> 0.01 us
  other arithmetic: 1 us -> 2.74 us
    unnamed x17 -> x6, local copies, waits for them, and re-layouts: 5.26 us -> 0.01 us
    pallas_call x1 -> x2, Pallas kernels: 97.7 us -> 103 us  [the longest x1 57.2 us: body(): pl.pallas_call(combine, out_shape=(jax.ShapeDtypeStruct((ROWS, C), F32),...]
    sub x1, other arithmetic: 1 us -> 2.14 us  [body(): new_global = global_weight - update]
where the time goes in v2:
time: 106 us
  Pallas kernels  103 us (97%)
  other arithmetic  2.74 us (3%)
    pallas_call x1, Pallas kernels, body(): pl.pallas_call(combine, out_shape=(jax.ShapeDtypeStruct((ROWS, C), F32),...  57.2 us
    pallas_call x1, Pallas kernels, body(): pl.pallas_call(encode, out_shape=jax.ShapeDtypeStruct((CHIPS, NCORE * BLK...  45.4 us
    sub x1, other arithmetic, body(): new_global = global_weight - update  2.14 us

profile of v2, /device:TPU:1, one launch (start us, length us, event | category | flops | bytes accessed | tf_op | source)
XLA Modules:
  0.0 106.1 jit_solution(2747678100577212855)
XLA Ops:
  0.6 0.0 copy-start
  0.6 45.4 %shard_map.86.code_out = bf16[32,48,128]{2,1,0:T(8,128)(2,1)} custom-call(bf16[128,3072]{1,0:T(8,128)(2,1)} %tok_hbm.1, bf16[128,1024]{1,0:T(8,128)(2,1)} %cot.1, f32[1,3072]{1,0:T(1,128)} %bitcast.9, f32[1,192,1024]{2,1,0:T(8,128)} %drift_hbm.1, s32[8,192]{1,0:T(8,128)} %bitcast.10), custom_call_target="tpu_custom_call" | custom-call | flops 805306368 | bytes 4194304 | tf_op jit(solution)/shard_map/pallas_call | solution.py:362
  46.1 57.2 %shard_map.87 = (f32[192,1024]{1,0:T(8,128)}, f32[24,128]{1,0:T(8,128)}) custom-call(bf16[32,48,128]{2,1,0:T(8,128)(2,1)} %shard_map.86.code_out, f32[24,128]{1,0:T(8,128)} %bitcast.6), custom_call_target="tpu_custom_call" | custom-call | flops 50331648 | bytes 2097152 | tf_op jit(solution)/shard_map/pallas_call | solution.py:390
  103.3 0.0 copy-done
  103.3 0.0 copy-start.1
  103.3 0.0 copy-start.2
  103.3 2.1 %sub.3 = f32[192,1024]{1,0:T(8,128)} subtract(f32[192,1024]{1,0:T(8,128)S(1)} %copy-done, f32[192,1024]{1,0:T(8,128)} %get-tuple-element.4) | non-fusion elementwise | flops 196608 | bytes 2359296 | tf_op jit(solution)/shard_map/sub | solution.py:409
  105.5 0.0 copy-done.1
  105.5 0.0 copy-done.2
  105.5 0.6 multiply_add_fusion
Async XLA Ops:
  0.6 102.7 %copy-start = (f32[192,1024]{1,0:T(8,128)S(1)}, f32[192,1024]{1,0:T(8,128)}, u32[]{:S(2)}) copy-start(f32[192,1024]{1,0:T(8,128)} %param.12) | copy-start | bytes 2359300
  103.3 2.2 %copy-start.1 = (f32[1,1,3,1024]{3,1,2,0:T(1,128)S(1)}, f32[1,1,3,1024]{3,1,2,0:T(1,128)}, u32[]{:S(2)}) copy-start(f32[1,1,3,1024]{3,1,2,0:T(1,128)} %param.13) | copy-start | bytes 36868
  103.3 2.2 %copy-start.2 = (f32[24,128]{1,0:T(8,128)S(1)}, f32[24,128]{1,0:T(8,128)}, u32[]{:S(2)}) copy-start(f32[24,128]{1,0:T(8,128)} %get-tuple-element.5) | copy-start | bytes 36868

commit v3 on v2

--- a/solution.py
+++ b/solution.py
@@ -26,7 +26,7 @@
 CW = C // PARTS
 GROUPS = 2 * FAR - 1
 UNIT = HD ** (-0.5)
-ENCODE_MIB, COMBINE_MIB = 60, 60
+KERNEL_MIB = 60
 
 
 def hadamard():
@@ -69,17 +69,23 @@
     pl.semaphore_signal(barrier, inc=1, device_id=device, device_id_type=pl.DeviceIdType.MESH)
 
 
-def encode(tok_hbm, cot, gain_hbm, drift_hbm, expo_hbm, code_out,
-           tok, gain, drift, expo, l_s, nt, lhs, cot2, y_out, y_in, grad, base, limit, squares, codes,
-           x_ss, x_rs, y_ss, y_rs, q_ss, q_rs):
-    rep, f, _, _, _, _ = place()
+def kernel(tok_hbm, cot, gain_hbm, drift_hbm, expo_hbm, mom_hbm, upd_out, delta_out,
+           tok, gain, drift, expo, mom, l_s, nt, lhs, cot2, y_out, y_in, grad, base, limit, squares, codes,
+           code_out, code_in, own_sum, sib_sum, upd,
+           x_ss, x_rs, y_ss, y_rs, q_ss, q_rs, c_ss, c_rs, s_ss, s_rs, a_ss, a_rs, b_ss, b_rs, h_ss, h_rs):
+    rep, f, core, chip, z, xh = place()
     y, x = f // NX, lax.rem(f, NX)
+
+    def rep_of(xh_, z_, core_):
+        return (xh_ * NZ + z_) * NCORE + core_
+
+    sibling = at(rep_of(xh, z, 1 - core), f)
 
     def cot_load(p):
         return pltpu.make_async_copy(cot.at[:, p * CW:(p + 1) * CW], cot2.at[p, :TOK, :], l_s.at[p])
 
     loads = [pltpu.make_async_copy(src, dst, l_s.at[PARTS + i]) for i, (src, dst) in enumerate(
-        ((tok_hbm, tok), (gain_hbm, gain), (drift_hbm, drift), (expo_hbm, expo)))]
+        ((tok_hbm, tok), (gain_hbm, gain), (drift_hbm, drift), (expo_hbm, expo), (mom_hbm, mom)))]
     loads[0].start()
     loads[1].start()
     for p in range(PARTS):
@@ -93,8 +99,14 @@
         greet(barrier, at(rep, lax.rem(f + i, N_FSDP)))
         return carry
 
+    def greet_r(i, carry):
+        greet(barrier, at(lax.rem(rep + NCORE * i, N_REP), f))
+        return carry
+
     lax.fori_loop(1, N_FSDP, greet_f, 0)
-    pl.semaphore_wait(barrier, N_FSDP - 1)
+    lax.fori_loop(1, CHIPS, greet_r, 0)
+    greet(barrier, sibling)
+    pl.semaphore_wait(barrier, N_FSDP - 1 + CHIPS)
 
     partner = at(rep, f + 1 - 2 * x)
 
@@ -231,46 +243,27 @@
     square = jnp.sum(jnp.sum(squares[...], axis=0), keepdims=True)
     factor = jnp.minimum(1.0, 1.0 / jnp.sqrt(square * (1.0 / (D * C)) + 1e-06))
 
-    for k in range(KVH):
-        cols = slice(k * HD, (k + 1) * HD)
-        bound = limit[:, cols]
-        codes[pl.ds(k, ROWS, stride=KVH), :] = jnp.clip(base[:, cols] + factor * grad[:, cols], -bound, bound)
-    code_out[...] = codes[...].reshape(CHIPS, NCORE * BLK, HD).astype(BF16)
-
-
-def combine(code_out, mom, upd_out, delta_out,
-            code_in, own_sum, sib_sum, upd, c_ss, c_rs, s_ss, s_rs, a_ss, a_rs, b_ss, b_rs, h_ss, h_rs):
-    rep, f, core, chip, z, xh = place()
-
-    def rep_of(xh_, z_, core_):
-        return (xh_ * NZ + z_) * NCORE + core_
-
-    barrier = pltpu.get_barrier_semaphore()
-
-    def greet_r(i, carry):
-        greet(barrier, at(lax.rem(rep + NCORE * i, N_REP), f))
-        return carry
-
-    lax.fori_loop(1, CHIPS, greet_r, 0)
-    sibling = at(rep_of(xh, z, 1 - core), f)
-    greet(barrier, sibling)
-    pl.semaphore_wait(barrier, CHIPS)
-
-    def c_start(i, carry):
-        there = lax.rem(xh + lax.rem(i // NZ + 2, NXH), NXH) * NZ + lax.rem(z + i, NZ)
-
-        @pl.when(there != chip)
-        def _():
+    group_rows = ROWS // NXH
+    for dx in (2, 3, 1, 0):
+        xx = lax.rem(xh + dx, NXH)
+        some = pl.ds(pl.multiple_of(xx * group_rows, group_rows), group_rows)
+        for k in range(KVH):
+            cols = slice(k * HD, (k + 1) * HD)
+            bound = limit[some, cols]
+            value = base[some, cols] + factor * grad[some, cols]
+            codes[dx, pl.ds(k, group_rows, stride=KVH), :] = jnp.clip(value, -bound, bound)
+        code_out[pl.ds(xx * NZ, NZ)] = codes[dx].reshape(NZ, NCORE * BLK, HD).astype(BF16)
+
+        def c_start(i, carry):
+            there = xx * NZ + lax.rem(z + i, NZ)
             remote(code_out.at[there], code_in.at[chip], c_ss.at[0], c_rs.at[0], at(there * NCORE + core, f)).start()
-
-        return carry
-
-    lax.fori_loop(0, CHIPS, c_start, 0)
-    own_code = pltpu.make_async_copy(code_out.at[chip], code_in.at[chip], s_ss.at[1])
-    own_code.start()
-    others = pl.ds(0, CHIPS - 1)
-    all_codes = remote(code_out.at[others], code_in.at[others], c_ss.at[0], c_rs.at[0], sibling)
-    own_code.wait()
+            return carry
+
+        lax.fori_loop(0 if dx else 1, NZ, c_start, 0)
+    code_in[chip] = code_out[chip]
+
+    chips = pl.ds(0, CHIPS - 1)
+    all_codes = remote(code_out.at[chips], code_in.at[chips], c_ss.at[0], c_rs.at[0], sibling)
     all_codes.wait_send()
     all_codes.wait_recv()
     summed = jnp.sum(code_in[...].astype(F32), axis=0)
@@ -279,7 +272,6 @@
     sib_copy = remote(own_sum.at[1 - core], sib_sum, s_ss.at[0], s_rs.at[0], sibling)
     sib_copy.start()
     sib_copy.wait()
-    signs = hadamard()
     mean_delta = rotate(own_sum[core] + sib_sum[...], signs, 3) * (UNIT / N_REP)
     new_momentum = momentum_decay * mom[...] + mean_delta
     upd[xh, z, core] = outer_rate * (mean_delta + momentum_decay * new_momentum)
@@ -359,17 +351,18 @@
     vmem = pl.BlockSpec(memory_space=pltpu.VMEM)
     hbm = pl.BlockSpec(memory_space=pl.ANY)
     own_rows = momentum.reshape(BLK, HD)
-    codes = pl.pallas_call(
-        encode,
-        out_shape=jax.ShapeDtypeStruct((CHIPS, NCORE * BLK, HD), BF16),
-        in_specs=[hbm] * 5,
-        out_specs=vmem,
+    update, mean_delta = pl.pallas_call(
+        kernel,
+        out_shape=(jax.ShapeDtypeStruct((ROWS, C), F32), jax.ShapeDtypeStruct((BLK, HD), F32)),
+        in_specs=[hbm] * 6,
+        out_specs=(vmem, vmem),
         scratch_shapes=[
             pltpu.VMEM((TOK, D), BF16),
             pltpu.VMEM((1, D), F32),
             pltpu.VMEM((1, ROWS, C), F32),
             pltpu.VMEM((KVH, ROWS), jnp.int32),
-            dma((PARTS + 4,)),
+            pltpu.VMEM((BLK, HD), F32),
+            dma((PARTS + 5,)),
             pltpu.VMEM((D, TOK), BF16),
             pltpu.VMEM((NY, ROWS, NX * TOK), BF16),
             pltpu.VMEM((PARTS, NX * TOK, CW), BF16),
@@ -379,33 +372,24 @@
             pltpu.VMEM((ROWS, C), F32),
             pltpu.VMEM((ROWS, C), F32),
             pltpu.VMEM((N_FSDP, 8, HD), F32),
-            pltpu.VMEM((ROWS * KVH, HD), F32),
-            dma((PARTS + NY,)), dma((PARTS + NY,)),
-            dma((2,)), dma((2, GROUPS, PARTS)),
-            dma((1,)), dma((1,)),
-        ],
-        compiler_params=pltpu.CompilerParams(collective_id=0, has_side_effects=True, vmem_limit_bytes=ENCODE_MIB * 2 ** 20),
-        cost_estimate=pl.CostEstimate(flops=2 * TOK * D * C, bytes_accessed=4 * 1024 * 1024, transcendentals=0),
-    )(tokens, cotangent, norm_gain.reshape(1, D), replica_drift, exponents[0].T)
-    update, mean_delta = pl.pallas_call(
-        combine,
-        out_shape=(jax.ShapeDtypeStruct((ROWS, C), F32), jax.ShapeDtypeStruct((BLK, HD), F32)),
-        in_specs=[hbm, vmem],
-        out_specs=(vmem, vmem),
-        scratch_shapes=[
+            pltpu.VMEM((NXH, ROWS // NXH * KVH, HD), F32),
+            pltpu.VMEM((CHIPS, NCORE * BLK, HD), BF16),
             pltpu.VMEM((CHIPS, NCORE * BLK, HD), BF16),
             pltpu.VMEM((NCORE, BLK, HD), F32),
             pltpu.VMEM((BLK, HD), F32),
             pltpu.VMEM((NXH, NZ, NCORE, BLK, HD), F32),
+            dma((PARTS + NY,)), dma((PARTS + NY,)),
+            dma((2,)), dma((2, GROUPS, PARTS)),
             dma((1,)), dma((1,)),
-            dma((2,)), dma((1,)),
+            dma((1,)), dma((1,)),
+            dma((1,)), dma((1,)),
             dma((NZ,)), dma((NZ,)),
             dma((NZ,)), dma((NZ,)),
             dma((NZ,)), dma((NZ,)),
         ],
-        compiler_params=pltpu.CompilerParams(collective_id=1, has_side_effects=True, vmem_limit_bytes=COMBINE_MIB * 2 ** 20),
-        cost_estimate=pl.CostEstimate(flops=2 * ROWS * C * HD, bytes_accessed=2 * 1024 * 1024, transcendentals=0),
-    )(codes, own_rows)
+        compiler_params=pltpu.CompilerParams(collective_id=0, has_side_effects=True, vmem_limit_bytes=KERNEL_MIB * 2 ** 20),
+        cost_estimate=pl.CostEstimate(flops=2 * TOK * D * C, bytes_accessed=4 * 1024 * 1024, transcendentals=0),
+    )(tokens, cotangent, norm_gain.reshape(1, D), replica_drift, exponents[0].T, own_rows)
     new_global = global_weight - update
     new_momentum = momentum_decay * own_rows + mean_delta
     return new_global, new_momentum.reshape(momentum.shape)

time: 106 us -> 99.5 us (0.939)
  Pallas kernels: 103 us -> 96 us
    pallas_call x2 -> x1, Pallas kernels: 103 us -> 96 us  [body(): pl.pallas_call(kernel, out_shape=(jax.ShapeDtypeStruct((ROWS, C), F32), j...]
where the time goes in v3:
time: 99.5 us; the launch traced here: 99.4 us
  Pallas kernels  96 us (96%)
  other arithmetic  2.74 us (3%)
    pallas_call x1, Pallas kernels, body(): pl.pallas_call(kernel, out_shape=(jax.ShapeDtypeStruct((ROWS, C), F32), j...  96 us
    sub x1, other arithmetic, body(): new_global = global_weight - update  2.14 us

profile of v3, /device:TPU:1, one launch (start us, length us, event | category | flops | bytes accessed | tf_op | source)
XLA Modules:
  0.0 99.4 jit_solution(10106104500173026402)
XLA Ops:
  0.6 0.0 copy-start
  0.6 96.0 %shard_map.86 = (f32[192,1024]{1,0:T(8,128)}, f32[24,128]{1,0:T(8,128)}) custom-call(bf16[128,3072]{1,0:T(8,128)(2,1)} %tok_hbm.1, bf16[128,1024]{1,0:T(8,128)(2,1)} %cot.1, f32[1,3072]{1,0:T(1,128)} %bitcast.9, f32[1,192,1024]{2,1,0:T(8,128)} %drift_hbm.1, s32[8,192]{1,0:T(8,128)} %bitcast.10, f32[24,128]{1,0:T(8,128)} %bitcast.6), custom_call_target="tpu_custom_call" | custom-call | flops 805306368 | bytes 4194304 | tf_op jit(solution)/shard_map/pallas_call | solution.py:354
  96.6 0.0 copy-done
  96.6 0.0 copy-start.1
  96.6 0.0 copy-start.2
  96.6 2.1 %sub.3 = f32[192,1024]{1,0:T(8,128)} subtract(f32[192,1024]{1,0:T(8,128)S(1)} %copy-done, f32[192,1024]{1,0:T(8,128)} %get-tuple-element.4) | non-fusion elementwise | flops 196608 | bytes 2359296 | tf_op jit(solution)/shard_map/sub | solution.py:393
  98.8 0.0 copy-done.1
  98.8 0.0 copy-done.2
  98.8 0.6 multiply_add_fusion
Async XLA Ops:
  0.6 96.0 %copy-start = (f32[192,1024]{1,0:T(8,128)S(1)}, f32[192,1024]{1,0:T(8,128)}, u32[]{:S(2)}) copy-start(f32[192,1024]{1,0:T(8,128)} %param.12) | copy-start | bytes 2359300
  96.6 2.2 %copy-start.1 = (f32[1,1,3,1024]{3,1,2,0:T(1,128)S(1)}, f32[1,1,3,1024]{3,1,2,0:T(1,128)}, u32[]{:S(2)}) copy-start(f32[1,1,3,1024]{3,1,2,0:T(1,128)} %param.13) | copy-start | bytes 36868
  96.6 2.2 %copy-start.2 = (f32[24,128]{1,0:T(8,128)S(1)}, f32[24,128]{1,0:T(8,128)}, u32[]{:S(2)}) copy-start(f32[24,128]{1,0:T(8,128)} %get-tuple-element.5) | copy-start | bytes 36868

commit v4 on v3

--- a/solution.py
+++ b/solution.py
@@ -69,8 +69,8 @@
     pl.semaphore_signal(barrier, inc=1, device_id=device, device_id_type=pl.DeviceIdType.MESH)
 
 
-def kernel(tok_hbm, cot, gain_hbm, drift_hbm, expo_hbm, mom_hbm, upd_out, delta_out,
-           tok, gain, drift, expo, mom, l_s, nt, lhs, cot2, y_out, y_in, grad, base, limit, squares, codes,
+def kernel(tok_hbm, cot, gain_hbm, drift_hbm, expo_hbm, mom_hbm, weight_hbm, new_out, momentum_out,
+           tok, gain, drift, expo, mom, weight, l_s, nt, lhs, cot2, y_out, y_in, grad, base, limit, squares, codes,
            code_out, code_in, own_sum, sib_sum, upd,
            x_ss, x_rs, y_ss, y_rs, q_ss, q_rs, c_ss, c_rs, s_ss, s_rs, a_ss, a_rs, b_ss, b_rs, h_ss, h_rs):
     rep, f, core, chip, z, xh = place()
@@ -85,7 +85,7 @@
         return pltpu.make_async_copy(cot.at[:, p * CW:(p + 1) * CW], cot2.at[p, :TOK, :], l_s.at[p])
 
     loads = [pltpu.make_async_copy(src, dst, l_s.at[PARTS + i]) for i, (src, dst) in enumerate(
-        ((tok_hbm, tok), (gain_hbm, gain), (drift_hbm, drift), (expo_hbm, expo), (mom_hbm, mom)))]
+        ((tok_hbm, tok), (gain_hbm, gain), (drift_hbm, drift), (expo_hbm, expo), (mom_hbm, mom), (weight_hbm, weight)))]
     loads[0].start()
     loads[1].start()
     for p in range(PARTS):
@@ -342,8 +342,9 @@
 
     flat = upd.reshape(ROWS * KVH, HD)
     for k in range(KVH):
-        upd_out[:, k * HD:(k + 1) * HD] = flat[pl.ds(k, ROWS, stride=KVH), :]
-    delta_out[...] = mean_delta
+        cols = slice(k * HD, (k + 1) * HD)
+        new_out[:, cols] = weight[:, cols] - flat[pl.ds(k, ROWS, stride=KVH), :]
+    momentum_out[...] = new_momentum
 
 
 def body(tokens, cotangent, norm_gain, replica_drift, exponents, global_weight, momentum):
@@ -351,10 +352,10 @@
     vmem = pl.BlockSpec(memory_space=pltpu.VMEM)
     hbm = pl.BlockSpec(memory_space=pl.ANY)
     own_rows = momentum.reshape(BLK, HD)
-    update, mean_delta = pl.pallas_call(
+    new_global, new_momentum = pl.pallas_call(
         kernel,
         out_shape=(jax.ShapeDtypeStruct((ROWS, C), F32), jax.ShapeDtypeStruct((BLK, HD), F32)),
-        in_specs=[hbm] * 6,
+        in_specs=[hbm] * 7,
         out_specs=(vmem, vmem),
         scratch_shapes=[
             pltpu.VMEM((TOK, D), BF16),
@@ -362,7 +363,8 @@
             pltpu.VMEM((1, ROWS, C), F32),
             pltpu.VMEM((KVH, ROWS), jnp.int32),
             pltpu.VMEM((BLK, HD), F32),
-            dma((PARTS + 5,)),
+            pltpu.VMEM((ROWS, C), F32),
+            dma((PARTS + 6,)),
             pltpu.VMEM((D, TOK), BF16),
             pltpu.VMEM((NY, ROWS, NX * TOK), BF16),
             pltpu.VMEM((PARTS, NX * TOK, CW), BF16),
@@ -389,9 +391,7 @@
         ],
         compiler_params=pltpu.CompilerParams(collective_id=0, has_side_effects=True, vmem_limit_bytes=KERNEL_MIB * 2 ** 20),
         cost_estimate=pl.CostEstimate(flops=2 * TOK * D * C, bytes_accessed=4 * 1024 * 1024, transcendentals=0),
-    )(tokens, cotangent, norm_gain.reshape(1, D), replica_drift, exponents[0].T, own_rows)
-    new_global = global_weight - update
-    new_momentum = momentum_decay * own_rows + mean_delta
+    )(tokens, cotangent, norm_gain.reshape(1, D), replica_drift, exponents[0].T, own_rows, global_weight)
     return new_global, new_momentum.reshape(momentum.shape)
 
 

time: 99.5 us -> 99.4 us (level)
  other arithmetic: 2.74 us -> 0 us
  local copies, waits for them, and re-layouts: 0.01 us -> 2.7 us
    unnamed x6 -> x4, local copies, waits for them, and re-layouts: 0.01 us -> 2.7 us
    sub x1 -> x0, other arithmetic: 2.14 us -> none  [body(): new_global = global_weight - update]
where the time goes in v4:
time: 99.4 us; the launch traced here: 99.2 us
  Pallas kernels  95.9 us (96%)
  local copies, waits for them, and re-layouts  2.7 us (3%)
    pallas_call x1, Pallas kernels, body(): pl.pallas_call(kernel, out_shape=(jax.ShapeDtypeStruct((ROWS, C), F32), j...  95.9 us
    unnamed x4, local copies, waits for them, and re-layouts  2.7 us

profile of v4, /device:TPU:1, one launch (start us, length us, event | category | flops | bytes accessed | tf_op | source)
XLA Modules:
  0.0 99.2 jit_solution(7622869522517377802)
XLA Ops:
  0.6 95.9 %shard_map.86 = (f32[192,1024]{1,0:T(8,128)}, f32[24,128]{1,0:T(8,128)}) custom-call(bf16[128,3072]{1,0:T(8,128)(2,1)} %tok_hbm.1, bf16[128,1024]{1,0:T(8,128)(2,1)} %cot.1, f32[1,3072]{1,0:T(1,128)} %bitcast.7, f32[1,192,1024]{2,1,0:T(8,128)} %drift_hbm.1, s32[8,192]{1,0:T(8,128)} %bitcast.9, f32[24,128]{1,0:T(8,128)} %bitcast.8, f32[192,1024]{1,0:T(8,128)} %weight_hbm.1), custom_call_target="tpu_custom_call" | custom-call | flops 805306368 | bytes 4194304 | tf_op jit(solution)/shard_map/pallas_call | solution.py:355
  96.5 0.0 copy-start
  96.5 2.1 %copy.13 = f32[192,1024]{1,0:T(8,128)} copy(f32[192,1024]{1,0:T(8,128)} %get-tuple-element.12) | data formatting | bytes 1572864
  98.6 0.0 copy-done
  98.6 0.6 copy.14
Async XLA Ops:
  96.5 2.1 %copy-start = (f32[24,128]{1,0:T(8,128)S(1)}, f32[24,128]{1,0:T(8,128)}, u32[]{:S(2)}) copy-start(f32[24,128]{1,0:T(8,128)} %get-tuple-element.5) | copy-start | bytes 36868
